TPU v7x, 256 devices: a whole 4x4x8 slice. The times are simulated.
256 devices in a mesh: fsdp: 16 (over z, core), slab: 8 (over y, x_lo), rep: 2 (over x_hi).
Axes of the slice: x: 4 (x_hi: 2, x_lo: 2; x = x_hi * 2 + x_lo), y: 4, z: 8, core: 2. Of those that a mesh axis runs over, the one named last changes fastest.
Arguments:
- inputs: bfloat16 [32, 32, 8, 8, 256], P(('fsdp', 'rep'), 'slab'), may hold values from -6 to 6
- weights: bfloat16 [256, 27, 256], P('fsdp'), may hold values from -0.078125 to 0.078125
- upstream: bfloat16 [32, 32, 8, 8, 256], P(('fsdp', 'rep'), 'slab'), may hold values from -6 to 6
Outputs:
- activated: bfloat16 [32, 32, 8, 8, 256], P(('fsdp', 'rep'), 'slab')
- input_grad: bfloat16 [32, 32, 8, 8, 256], P(('fsdp', 'rep'), 'slab')
- weight_grad: float32 [256, 27, 256], P('fsdp')
All inputs are finite; a program needn't handle non-finite values.
Results may differ from a plain program's by a relative error of at most 0.0049.
Values may be sent and summed in bfloat16 or wider, within the bound.
No kernel may reach another device: no remote copies, remote signals or barrier semaphores. Data moves between devices by JAX's collectives and lax.ppermute only.
A program may use at most 256 MiB of HBM per device.

v0:
```python
import jax
import jax.numpy as jnp
from jax import lax
from jax.sharding import PartitionSpec as P


def padded_2(cells, sides, width):
    for axis, dim in sides:
        count = lax.axis_size(axis)
        ends = count - 1
        head = lax.slice_in_dim(cells, 0, width, axis=dim)
        tail = lax.slice_in_dim(cells, cells.shape[dim] - width, cells.shape[dim], axis=dim)
        cells = jnp.concatenate(
            [
                lax.ppermute(tail, axis, [(i, (i + 1) % count) for i in range(ends)]),
                cells,
                lax.ppermute(head, axis, [((i + 1) % count, i) for i in range(ends)]),
            ],
            axis=dim,
        )
    return cells


def silu_slope(preact):
    logistic = jax.nn.sigmoid(preact)
    return logistic * (1.0 + preact * (1.0 - logistic))


def pad_cross(field):
    return jnp.pad(field, ((0, 0), (0, 0), (1, 1), (1, 1), (0, 0)))


def grad_rim(field):
    return pad_cross(padded_2(field, (("slab", 1),), 1))


def tap_list():
    return [
        (along_x, along_y, along_z)
        for along_x in range(3)
        for along_y in range(3)
        for along_z in range(3)
    ]


def forward_rows(padded, weight_rows):
    planes = padded.shape[1] - 2
    height = padded.shape[2] - 2
    breadth = padded.shape[3] - 2
    total = None
    for index, (along_x, along_y, along_z) in enumerate(tap_list()):
        window = padded[
            :,
            along_x : along_x + planes,
            along_y : along_y + height,
            along_z : along_z + breadth,
            :,
        ]
        term = jnp.einsum(
            "bxyzi,oi->bxyzo", window, weight_rows[:, index, :], preferred_element_type=jnp.float32
        )
        total = term if total is None else total + term
    return total


def backward_rows(grads_pad, weight_rows):
    planes = grads_pad.shape[1] - 2
    height = grads_pad.shape[2] - 2
    breadth = grads_pad.shape[3] - 2
    total = None
    for index, (along_x, along_y, along_z) in enumerate(tap_list()):
        grad_window = grads_pad[
            :,
            2 - along_x : 2 - along_x + planes,
            2 - along_y : 2 - along_y + height,
            2 - along_z : 2 - along_z + breadth,
            :,
        ]
        term = jnp.einsum(
            "bxyzo,oi->bxyzi",
            grad_window,
            weight_rows[:, index, :],
            preferred_element_type=jnp.float32,
        )
        total = term if total is None else total + term
    return total


def weight_terms(grads, padded, factor):
    planes = grads.shape[1]
    height = grads.shape[2]
    breadth = grads.shape[3]
    stacked = []
    for along_x, along_y, along_z in tap_list():
        window = padded[
            :,
            along_x : along_x + planes,
            along_y : along_y + height,
            along_z : along_z + breadth,
            :,
        ]
        stacked.append(
            jnp.einsum("bxyzo,bxyzi->oi", grads, window, preferred_element_type=jnp.float32)
        )
    return jnp.stack(stacked, axis=1) * factor


def local(inputs, weights, upstream):
    samples = inputs.shape[0]
    planes = inputs.shape[1]
    height = inputs.shape[2]
    breadth = inputs.shape[3]
    total_cells = (
        samples
        * lax.axis_size("fsdp")
        * lax.axis_size("rep")
        * planes
        * lax.axis_size("slab")
        * height
        * breadth
    )
    factor = float(total_cells) ** (-0.5)
    inputs_halo = padded_2(inputs, (("slab", 1),), 1)
    inputs_pad = pad_cross(inputs_halo)
    whole = lax.all_gather(weights, "fsdp", axis=0, tiled=True)
    preact = forward_rows(inputs_pad, whole)
    activated = jax.nn.silu(preact).astype(jnp.bfloat16)
    grad_pre = (upstream.astype(jnp.float32) * silu_slope(preact)).astype(jnp.bfloat16)
    grads_pad = grad_rim(grad_pre)
    input_grad = backward_rows(grads_pad, whole).astype(jnp.bfloat16)
    terms = weight_terms(grad_pre, inputs_pad, factor)
    shard = lax.psum_scatter(terms, "fsdp", scatter_dimension=0, tiled=True)
    weight_grad = lax.psum(shard, ("slab", "rep"))
    return (activated, input_grad, weight_grad)


def solution(mesh):
    placed = (
        P(("fsdp", "rep"), "slab", None, None, None),
        P("fsdp", None, None),
        P(("fsdp", "rep"), "slab", None, None, None),
    )
    return jax.shard_map(
        local,
        mesh=mesh,
        in_specs=placed,
        out_specs=(
            P(("fsdp", "rep"), "slab", None, None, None),
            P(("fsdp", "rep"), "slab", None, None, None),
            P("fsdp", None, None),
        ),
        check_vma=False,
    )
```

profile of v0, /device:TPU:32, one launch (start us, length us, event | category | flops | bytes accessed | tf_op | source)
XLA Modules:
  0.0 247.4 jit_solution(10040391627877063961)
XLA Ops:
  8.7 3.4 %collective-permute-start = (bf16[1,1,8,8,256]{4,3,2,1,0:T(8,128)(2,1)S(1)}, bf16[1,1,8,8,256]{4,3,2,1,0:T(8,128)(2,1)S(1)}, u32[]{:S(2)}, u32[]{:S(2)}) collective-permute-start(bf16[1,1,8,8,256]{4,3,2,1,0:T(8,128)(2,1)S(1)} %get-tuple-element.5), channel_id=1, source_target_pairs={{0,2},{2,4},{4,6},{6,8},{8,10},{10,12},{12,14},{1,3},{3,5},{5,7},{... | collective-permute-start | bytes 98312 | tf_op jit(solution)/shard_map/ppermute | solution.py:15
  12.1 1.3 collective-permute-start.1
  13.7 4.2 %collective-permute-done.1 = bf16[1,1,8,8,256]{4,3,2,1,0:T(8,128)(2,1)S(1)} collective-permute-done((bf16[1,1,8,8,256]{4,3,2,1,0:T(8,128)(2,1)S(1)}, bf16[1,1,8,8,256]{4,3,2,1,0:T(8,128)(2,1)S(1)}, u32[]{:S(2)}, u32[]{:S(2)}) %collective-permute-start.1) | collective-permute-done | bytes 32800 | tf_op jit(solution)/shard_map/ppermute | solution.py:17
  19.0 34.5 %all-gather.2.cloned.1.call-done = bf16[256,27,256]{2,0,1:T(8,128)(2,1)} async-done(((bf16[16,27,256]{2,0,1:T(8,128)(2,1)}), bf16[256,27,256]{2,0,1:T(8,128)(2,1)}) %all-gather.2.cloned.1.call-update) | async-done | bytes 3538960 | tf_op jit(solution)/shard_map/all_gather | solution.py:125
  53.5 1.3 fusion.82
  54.8 1.1 fusion.81
  56.0 1.1 fusion.80
  57.1 1.1 convolution_add_fusion.47
  58.2 1.1 convolution_add_fusion.46
  59.4 1.1 convolution_add_fusion.45
  71.7 3.4 %broadcast_multiply_fusion = f32[256,27,256]{2,0,1:T(8,128)} fusion(f32[256,27,256]{2,0,1:T(8,128)S(1)} %fusion.4), kind=kLoop, calls=%fused_computation | loop fusion | flops 1769472 | bytes 14155776 | tf_op jit(solution)/shard_map/mul | solution.py:105
  75.2 3.6 %collective-permute-start.2 = (bf16[1,1,8,8,256]{4,3,2,1,0:T(8,128)(2,1)S(1)}, bf16[1,1,8,8,256]{4,3,2,1,0:T(8,128)(2,1)S(1)}, u32[]{:S(2)}, u32[]{:S(2)}) collective-permute-start(bf16[1,1,8,8,256]{4,3,2,1,0:T(8,128)(2,1)S(1)} %get-tuple-element.3), channel_id=1, source_target_pairs={{0,2},{2,4},{4,6},{6,8},{8,10},{10,12},{12,14},{1,3},{3,5},{5,7},{... | collective-permute-start | bytes 98312 | tf_op jit(solution)/shard_map/ppermute | solution.py:15
  78.8 1.3 collective-permute-start.3
  80.9 3.8 %collective-permute-done.3 = bf16[1,1,8,8,256]{4,3,2,1,0:T(8,128)(2,1)S(1)} collective-permute-done((bf16[1,1,8,8,256]{4,3,2,1,0:T(8,128)(2,1)S(1)}, bf16[1,1,8,8,256]{4,3,2,1,0:T(8,128)(2,1)S(1)}, u32[]{:S(2)}, u32[]{:S(2)}) %collective-permute-start.3) | collective-permute-done | bytes 32800 | tf_op jit(solution)/shard_map/ppermute | solution.py:17
  84.8 1.1 fusion.38
  85.9 1.1 fusion.42
  87.0 1.1 fusion.46
  88.1 1.1 convolution_add_fusion.23
  93.2 45.6 %reduce-scatter.2.cloned.1.call-done = f32[16,27,256]{2,0,1:T(8,128)} async-done(((f32[256,27,256]{2,0,1:T(8,128)}), f32[16,27,256]{2,0,1:T(8,128)}) %reduce-scatter.2.cloned.1.call-update) | async-done | bytes 442384 | tf_op jit(solution)/shard_map/reduce_scatter | solution.py:132
  138.9 1.1 convolution_add_fusion.2
  140.0 1.1 convolution_add_fusion.1
  141.1 1.8 fusion.32
  142.8 96.2 %all-reduce.4.cloned.1.call-done = f32[16,27,256]{2,0,1:T(8,128)} async-done(((f32[16,27,256]{2,0,1:T(8,128)}), f32[16,27,256]{2,0,1:T(8,128)}) %all-reduce.4.cloned.1.call-update) | async-done | bytes 442384 | tf_op jit(solution)/shard_map/psum | solution.py:133
  239.1 1.8 copy.87
  (89 shorter events, 18.6 us)
Async XLA Ops:
  7.2 53.3 %copy-start.2 = (bf16[1,4,8,8,256]{4,3,2,1,0:T(8,128)(2,1)S(1)}, bf16[1,4,8,8,256]{4,3,2,1,0:T(8,128)(2,1)}, u32[]{:S(2)}) copy-start(bf16[1,4,8,8,256]{4,3,2,1,0:T(8,128)(2,1)} %param.3) | copy-start | bytes 393220
  7.2 46.4 %all-gather.2.cloned.1.call-start = ((), (), s32[]{:S(2)}) async-start(), calls=%async_computation.1 | async-start | bytes 3760128 | tf_op jit(solution)/shard_map/all_gather | solution.py:125
  7.9 130.9 %reduce-scatter.2.cloned.1.call-start = ((), (), s32[]{:S(2)}) async-start(), calls=%async_computation.2 | async-start | bytes 7520256 | tf_op jit(solution)/shard_map/reduce_scatter | solution.py:132
  8.7 5.0 %collective-permute-start = (bf16[1,1,8,8,256]{4,3,2,1,0:T(8,128)(2,1)S(1)}, bf16[1,1,8,8,256]{4,3,2,1,0:T(8,128)(2,1)S(1)}, u32[]{:S(2)}, u32[]{:S(2)}) collective-permute-start(bf16[1,1,8,8,256]{4,3,2,1,0:T(8,128)(2,1)S(1)} %get-tuple-element.5), channel_id=1, source_target_pairs={{0,2},{2,4},{4,6},{6,8},{8,10},{10,12},{12,14},{1,3},{3,5},{5,7},{... | collective-permute-start | bytes 98312 | tf_op jit(solution)/shard_map/ppermute | solution.py:15
  12.1 5.8 %collective-permute-start.1 = (bf16[1,1,8,8,256]{4,3,2,1,0:T(8,128)(2,1)S(1)}, bf16[1,1,8,8,256]{4,3,2,1,0:T(8,128)(2,1)S(1)}, u32[]{:S(2)}, u32[]{:S(2)}) collective-permute-start(bf16[1,1,8,8,256]{4,3,2,1,0:T(8,128)(2,1)S(1)} %get-tuple-element.6), channel_id=1, source_target_pairs={{2,0},{4,2},{6,4},{8,6},{10,8},{12,10},{14,12},{3,1},{5,3},{7,5},{... | collective-permute-start | bytes 98312 | tf_op jit(solution)/shard_map/ppermute | solution.py:17
  53.5 7.0 %copy-start = (bf16[256,27,256]{2,0,1:T(8,128)(2,1)S(1)}, bf16[256,27,256]{2,0,1:T(8,128)(2,1)}, u32[]{:S(2)}) copy-start(bf16[256,27,256]{2,0,1:T(8,128)(2,1)} %all-gather.2.cloned.1.call-done) | copy-start | bytes 10616836
  63.1 2.1 copy-start.3
  75.1 163.9 %all-reduce.4.cloned.1.call-start = ((), (), s32[]{:S(2)}) async-start(), calls=%async_computation.3 | async-start | bytes 884736 | tf_op jit(solution)/shard_map/psum | solution.py:133
  75.2 14.1 %copy-start.1 = (bf16[256,27,256]{2,0,1:T(8,128)(2,1)S(1)}, bf16[256,27,256]{2,0,1:T(8,128)(2,1)}, u32[]{:S(2)}) copy-start(bf16[256,27,256]{2,0,1:T(8,128)(2,1)} %all-gather.2.cloned.1.call-done) | copy-start | bytes 10616836
  75.2 5.7 %collective-permute-start.2 = (bf16[1,1,8,8,256]{4,3,2,1,0:T(8,128)(2,1)S(1)}, bf16[1,1,8,8,256]{4,3,2,1,0:T(8,128)(2,1)S(1)}, u32[]{:S(2)}, u32[]{:S(2)}) collective-permute-start(bf16[1,1,8,8,256]{4,3,2,1,0:T(8,128)(2,1)S(1)} %get-tuple-element.3), channel_id=1, source_target_pairs={{0,2},{2,4},{4,6},{6,8},{8,10},{10,12},{12,14},{1,3},{3,5},{5,7},{... | collective-permute-start | bytes 98312 | tf_op jit(solution)/shard_map/ppermute | solution.py:15
  78.8 5.8 %collective-permute-start.3 = (bf16[1,1,8,8,256]{4,3,2,1,0:T(8,128)(2,1)S(1)}, bf16[1,1,8,8,256]{4,3,2,1,0:T(8,128)(2,1)S(1)}, u32[]{:S(2)}, u32[]{:S(2)}) collective-permute-start(bf16[1,1,8,8,256]{4,3,2,1,0:T(8,128)(2,1)S(1)} %get-tuple-element.4), channel_id=1, source_target_pairs={{2,0},{4,2},{6,4},{8,6},{10,8},{12,10},{14,12},{3,1},{5,3},{7,5},{... | collective-permute-start | bytes 98312 | tf_op jit(solution)/shard_map/ppermute | solution.py:17
Sparse Core Ops, SparseCore 0:
  9.9 43.6 all-gather.1
  75.2 63.5 reduce-scatter.1
  142.4 96.5 all-reduce.3
where the time goes:
time: 248 us; the launch traced here: 247 us
  waiting for transfers between devices  185 us (75%)
  matrix products  30 us (12%)
  between operations  14.4 us (6%)
  starting transfers between devices  9.72 us (4%)
  other arithmetic  5.36 us (2%)
  local copies, waits for them, and re-layouts  2.61 us (1%)
    psum x1, waiting for transfers between devices, local(): weight_grad = lax.psum(shard, ('slab', 'rep'))  96.2 us
    reduce_scatter x1, waiting for transfers between devices, local(): shard = lax.psum_scatter(terms, 'fsdp', scatter_dimension=0, tiled=True)  45.6 us
    all_gather x1, waiting for transfers between devices, local(): whole = lax.all_gather(weights, 'fsdp', axis=0, tiled=True)  34.5 us
    dot_general x27, matrix products, backward_rows(): jnp.einsum('bxyzo,oi->bxyzi', grad_window, weight_rows[:, index, :], pref...  12.2 us
    dot_general x27, matrix products, forward_rows(): jnp.einsum('bxyzi,oi->bxyzo', window, weight_rows[:, index, :], preferred...  11.7 us
    ppermute x2, waiting for transfers between devices, padded_2(): lax.ppermute(head, axis, [((i + 1) % count, i) for i in range(ends)])  8 us
    ppermute x2, starting transfers between devices, padded_2(): lax.ppermute(tail, axis, [(i, (i + 1) % count) for i in range(ends)])  7.02 us
    dot_general x27, matrix products, weight_terms(): jnp.einsum('bxyzo,bxyzi->oi', grads, window, preferred_element_type=jnp.f...  6.1 us
  transfers between devices with their start and end apart: 7, of which 6 were waited for; matrix products, arithmetic and copies ran while one was open for 6% of the time, Pallas kernels for 0%

commit v1 on v0

--- a/solution.py
+++ b/solution.py
@@ -130,7 +130,7 @@
     input_grad = backward_rows(grads_pad, whole).astype(jnp.bfloat16)
     terms = weight_terms(grad_pre, inputs_pad, factor)
     shard = lax.psum_scatter(terms, "fsdp", scatter_dimension=0, tiled=True)
-    weight_grad = lax.psum(shard, ("slab", "rep"))
+    weight_grad = lax.psum(lax.psum(shard, "rep"), "slab")
     return (activated, input_grad, weight_grad)
 
 

time: 248 us -> 275 us (1.11)
  waiting for transfers between devices: 185 us -> 211 us
    psum x1 -> x2, waiting for transfers between devices: 96.2 us -> 121 us  [local(): weight_grad = lax.psum(lax.psum(shard, 'rep'), 'slab')]
  transfers between devices with their start and end apart: 7 -> 8, of which waited for: 6 -> 7; matrix products, arithmetic and copies ran while one was open for 6% -> 6% of each run, Pallas kernels for 0% -> 0%
where the time goes in v1:
time: 275 us
  waiting for transfers between devices  211 us (77%)
  matrix products  31.8 us (12%)
  between operations  14.4 us (5%)
  starting transfers between devices  9.76 us (4%)
  other arithmetic  5.36 us (2%)
    psum x2, waiting for transfers between devices, local(): weight_grad = lax.psum(lax.psum(shard, 'rep'), 'slab')  121 us
    reduce_scatter x1, waiting for transfers between devices, local(): shard = lax.psum_scatter(terms, 'fsdp', scatter_dimension=0, tiled=True)  46 us
    all_gather x1, waiting for transfers between devices, local(): whole = lax.all_gather(weights, 'fsdp', axis=0, tiled=True)  34.5 us
    dot_general x27, matrix products, backward_rows(): jnp.einsum('bxyzo,oi->bxyzi', grad_window, weight_rows[:, index, :], pref...  14 us
    dot_general x27, matrix products, forward_rows(): jnp.einsum('bxyzi,oi->bxyzo', window, weight_rows[:, index, :], preferred...  11.7 us
    ppermute x2, waiting for transfers between devices, padded_2(): lax.ppermute(head, axis, [((i + 1) % count, i) for i in range(ends)])  8 us
    ppermute x2, starting transfers between devices, padded_2(): lax.ppermute(tail, axis, [(i, (i + 1) % count) for i in range(ends)])  7.02 us
    dot_general x27, matrix products, weight_terms(): jnp.einsum('bxyzo,bxyzi->oi', grads, window, preferred_element_type=jnp.f...  6.1 us
  transfers between devices with their start and end apart: 8, of which 7 were waited for; matrix products, arithmetic and copies ran while one was open for 6% of the time, Pallas kernels for 0%

profile of v1, /device:TPU:32, one launch (start us, length us, event | category | flops | bytes accessed | tf_op | source)
XLA Modules:
  0.0 274.5 jit_solution(7858093793577027435)
XLA Ops:
  8.7 3.4 %collective-permute-start = (bf16[1,1,8,8,256]{4,3,2,1,0:T(8,128)(2,1)S(1)}, bf16[1,1,8,8,256]{4,3,2,1,0:T(8,128)(2,1)S(1)}, u32[]{:S(2)}, u32[]{:S(2)}) collective-permute-start(bf16[1,1,8,8,256]{4,3,2,1,0:T(8,128)(2,1)S(1)} %get-tuple-element.5), channel_id=1, source_target_pairs={{0,2},{2,4},{4,6},{6,8},{8,10},{10,12},{12,14},{1,3},{3,5},{5,7},{... | collective-permute-start | bytes 98312 | tf_op jit(solution)/shard_map/ppermute | solution.py:15
  12.1 1.3 collective-permute-start.1
  13.7 4.2 %collective-permute-done.1 = bf16[1,1,8,8,256]{4,3,2,1,0:T(8,128)(2,1)S(1)} collective-permute-done((bf16[1,1,8,8,256]{4,3,2,1,0:T(8,128)(2,1)S(1)}, bf16[1,1,8,8,256]{4,3,2,1,0:T(8,128)(2,1)S(1)}, u32[]{:S(2)}, u32[]{:S(2)}) %collective-permute-start.1) | collective-permute-done | bytes 32800 | tf_op jit(solution)/shard_map/ppermute | solution.py:17
  19.0 34.5 %all-gather.2.cloned.1.call-done = bf16[256,27,256]{2,0,1:T(8,128)(2,1)} async-done(((bf16[16,27,256]{2,0,1:T(8,128)(2,1)}), bf16[256,27,256]{2,0,1:T(8,128)(2,1)}) %all-gather.2.cloned.1.call-update) | async-done | bytes 3538960 | tf_op jit(solution)/shard_map/all_gather | solution.py:125
  53.5 1.3 fusion.82
  54.8 1.1 fusion.81
  56.0 1.1 fusion.80
  57.1 1.1 convolution_add_fusion.47
  58.2 1.1 convolution_add_fusion.46
  59.4 1.1 convolution_add_fusion.45
  71.7 3.4 %broadcast_multiply_fusion = f32[256,27,256]{2,0,1:T(8,128)} fusion(f32[256,27,256]{2,0,1:T(8,128)S(1)} %fusion.4), kind=kLoop, calls=%fused_computation | loop fusion | flops 1769472 | bytes 14155776 | tf_op jit(solution)/shard_map/mul | solution.py:105
  75.2 3.6 %collective-permute-start.2 = (bf16[1,1,8,8,256]{4,3,2,1,0:T(8,128)(2,1)S(1)}, bf16[1,1,8,8,256]{4,3,2,1,0:T(8,128)(2,1)S(1)}, u32[]{:S(2)}, u32[]{:S(2)}) collective-permute-start(bf16[1,1,8,8,256]{4,3,2,1,0:T(8,128)(2,1)S(1)} %get-tuple-element.3), channel_id=1, source_target_pairs={{0,2},{2,4},{4,6},{6,8},{8,10},{10,12},{12,14},{1,3},{3,5},{5,7},{... | collective-permute-start | bytes 98312 | tf_op jit(solution)/shard_map/ppermute | solution.py:15
  78.8 1.3 collective-permute-start.3
  80.9 3.8 %collective-permute-done.3 = bf16[1,1,8,8,256]{4,3,2,1,0:T(8,128)(2,1)S(1)} collective-permute-done((bf16[1,1,8,8,256]{4,3,2,1,0:T(8,128)(2,1)S(1)}, bf16[1,1,8,8,256]{4,3,2,1,0:T(8,128)(2,1)S(1)}, u32[]{:S(2)}, u32[]{:S(2)}) %collective-permute-start.3) | collective-permute-done | bytes 32800 | tf_op jit(solution)/shard_map/ppermute | solution.py:17
  84.8 1.1 fusion.42
  87.0 1.1 convolution_add_fusion.23
  88.1 1.1 convolution_add_fusion.22
  92.9 46.0 %reduce-scatter.2.cloned.1.call-done = f32[16,27,256]{2,0,1:T(8,128)} async-done(((f32[256,27,256]{2,0,1:T(8,128)}), f32[16,27,256]{2,0,1:T(8,128)}) %reduce-scatter.2.cloned.1.call-update) | async-done | bytes 442384 | tf_op jit(solution)/shard_map/reduce_scatter | solution.py:132
  140.0 1.1 fusion
  141.1 42.7 %all-reduce.5.cloned.1.call-done = f32[16,27,256]{2,0,1:T(8,128)} async-done(((f32[16,27,256]{2,0,1:T(8,128)}), f32[16,27,256]{2,0,1:T(8,128)}) %all-reduce.5.cloned.1.call-update) | async-done | bytes 442384 | tf_op jit(solution)/shard_map/psum | solution.py:133
  183.8 1.1 convolution_add_fusion.2
  186.0 1.8 fusion.32
  187.8 78.4 %all-reduce.7.cloned.1.call-done = f32[16,27,256]{2,0,1:T(8,128)} async-done(((f32[16,27,256]{2,0,1:T(8,128)}), f32[16,27,256]{2,0,1:T(8,128)}) %all-reduce.7.cloned.1.call-update) | async-done | bytes 442384 | tf_op jit(solution)/shard_map/psum | solution.py:133
  266.2 1.8 copy.88
  (92 shorter events, 21.6 us)
Async XLA Ops:
  7.2 53.3 %copy-start.2 = (bf16[1,4,8,8,256]{4,3,2,1,0:T(8,128)(2,1)S(1)}, bf16[1,4,8,8,256]{4,3,2,1,0:T(8,128)(2,1)}, u32[]{:S(2)}) copy-start(bf16[1,4,8,8,256]{4,3,2,1,0:T(8,128)(2,1)} %param.3) | copy-start | bytes 393220
  7.2 46.4 %all-gather.2.cloned.1.call-start = ((), (), s32[]{:S(2)}) async-start(), calls=%async_computation.1 | async-start | bytes 3760128 | tf_op jit(solution)/shard_map/all_gather | solution.py:125
  7.9 130.9 %reduce-scatter.2.cloned.1.call-start = ((), (), s32[]{:S(2)}) async-start(), calls=%async_computation.2 | async-start | bytes 7520256 | tf_op jit(solution)/shard_map/reduce_scatter | solution.py:132
  8.7 5.0 %collective-permute-start = (bf16[1,1,8,8,256]{4,3,2,1,0:T(8,128)(2,1)S(1)}, bf16[1,1,8,8,256]{4,3,2,1,0:T(8,128)(2,1)S(1)}, u32[]{:S(2)}, u32[]{:S(2)}) collective-permute-start(bf16[1,1,8,8,256]{4,3,2,1,0:T(8,128)(2,1)S(1)} %get-tuple-element.5), channel_id=1, source_target_pairs={{0,2},{2,4},{4,6},{6,8},{8,10},{10,12},{12,14},{1,3},{3,5},{5,7},{... | collective-permute-start | bytes 98312 | tf_op jit(solution)/shard_map/ppermute | solution.py:15
  12.1 5.8 %collective-permute-start.1 = (bf16[1,1,8,8,256]{4,3,2,1,0:T(8,128)(2,1)S(1)}, bf16[1,1,8,8,256]{4,3,2,1,0:T(8,128)(2,1)S(1)}, u32[]{:S(2)}, u32[]{:S(2)}) collective-permute-start(bf16[1,1,8,8,256]{4,3,2,1,0:T(8,128)(2,1)S(1)} %get-tuple-element.6), channel_id=1, source_target_pairs={{2,0},{4,2},{6,4},{8,6},{10,8},{12,10},{14,12},{3,1},{5,3},{7,5},{... | collective-permute-start | bytes 98312 | tf_op jit(solution)/shard_map/ppermute | solution.py:17
  53.5 7.0 %copy-start = (bf16[256,27,256]{2,0,1:T(8,128)(2,1)S(1)}, bf16[256,27,256]{2,0,1:T(8,128)(2,1)}, u32[]{:S(2)}) copy-start(bf16[256,27,256]{2,0,1:T(8,128)(2,1)} %all-gather.2.cloned.1.call-done) | copy-start | bytes 10616836
  63.1 2.1 copy-start.3
  75.1 108.7 %all-reduce.5.cloned.1.call-start = ((), (), s32[]{:S(2)}) async-start(), calls=%async_computation.3 | async-start | bytes 884736 | tf_op jit(solution)/shard_map/psum | solution.py:133
  75.2 14.1 %copy-start.1 = (bf16[256,27,256]{2,0,1:T(8,128)(2,1)S(1)}, bf16[256,27,256]{2,0,1:T(8,128)(2,1)}, u32[]{:S(2)}) copy-start(bf16[256,27,256]{2,0,1:T(8,128)(2,1)} %all-gather.2.cloned.1.call-done) | copy-start | bytes 10616836
  75.2 5.7 %collective-permute-start.2 = (bf16[1,1,8,8,256]{4,3,2,1,0:T(8,128)(2,1)S(1)}, bf16[1,1,8,8,256]{4,3,2,1,0:T(8,128)(2,1)S(1)}, u32[]{:S(2)}, u32[]{:S(2)}) collective-permute-start(bf16[1,1,8,8,256]{4,3,2,1,0:T(8,128)(2,1)S(1)} %get-tuple-element.3), channel_id=1, source_target_pairs={{0,2},{2,4},{4,6},{6,8},{8,10},{10,12},{12,14},{1,3},{3,5},{5,7},{... | collective-permute-start | bytes 98312 | tf_op jit(solution)/shard_map/ppermute | solution.py:15
  78.8 5.8 %collective-permute-start.3 = (bf16[1,1,8,8,256]{4,3,2,1,0:T(8,128)(2,1)S(1)}, bf16[1,1,8,8,256]{4,3,2,1,0:T(8,128)(2,1)S(1)}, u32[]{:S(2)}, u32[]{:S(2)}) collective-permute-start(bf16[1,1,8,8,256]{4,3,2,1,0:T(8,128)(2,1)S(1)} %get-tuple-element.4), channel_id=1, source_target_pairs={{2,0},{4,2},{6,4},{8,6},{10,8},{12,10},{14,12},{3,1},{5,3},{7,5},{... | collective-permute-start | bytes 98312 | tf_op jit(solution)/shard_map/ppermute | solution.py:17
  138.9 127.3 %all-reduce.7.cloned.1.call-start = ((), (), s32[]{:S(2)}) async-start(), calls=%async_computation.4 | async-start | bytes 884736 | tf_op jit(solution)/shard_map/psum | solution.py:133
Sparse Core Ops, SparseCore 0:
  9.9 43.6 all-gather.1
  75.2 63.5 reduce-scatter.1
  141.6 42.0 all-reduce.4
  186.3 79.8 all-reduce.6
